TPU v7x, 32 devices: a whole 2x2x4 slice. The times are simulated.
32 devices in a mesh: row: 8 (over z, core), col: 4 (over y, x).
Axes of the slice: x: 2, y: 2, z: 4, core: 2. Of those that a mesh axis runs over, the one named last changes fastest.
Arguments:
- weights: bfloat16 [2, 24576, 6144], P(None, 'row', 'col'), may hold values from -0.109375 to 0.109375
- pattern: int32 [2, 192, 48], P(None, 'row', 'col'), may hold values 0 or 1
- sketch: bfloat16 [6144, 512], P('col'), may hold values from -6 to 6
Outputs:
- basis: float32 [2, 24576, 512], P(None, ('row', 'col'))
Inputs may be any that keep to these rules, and one draw needn't show every extreme that they name: `pattern`: 1 marks a block of the sparse part, 0 a block of the residual.
All inputs are finite; a program needn't handle non-finite values.
Results may differ from a plain program's by a relative error of at most 0.0003.
Values sent between devices are 32-bit elements; how exact they have to be, the bound alone decides.
A program may use at most 128 MiB of HBM per device.

v0:
```python
import jax
import jax.numpy as jnp
from jax import lax
from jax.sharding import PartitionSpec as P

M = 24576
BLOCK = 128
LAYERS = 2


def make_basis(rows_here, gram):
    lower = jnp.linalg.cholesky(gram)
    solved = lax.linalg.triangular_solve(
        lower, rows_here, left_side=False, lower=True, transpose_a=True
    )
    return solved * jnp.sqrt(jnp.float32(M))


def local_gram(rows_here):
    return lax.dot_general(
        rows_here,
        rows_here,
        (((0,), (0,)), ((), ())),
        precision=lax.Precision.HIGHEST,
        preferred_element_type=jnp.float32,
    )


def body(weights, pattern, sketch):
    row_count = weights.shape[1]
    col_count = weights.shape[2]
    outputs = []
    for layer in range(LAYERS):
        keep = (1 - pattern[layer]).astype(jnp.bfloat16)
        shaped = (
            weights[layer].reshape(row_count // BLOCK, BLOCK, col_count // BLOCK, BLOCK)
            * keep[:, None, :, None]
        )
        leftover = shaped.reshape(row_count, col_count)
        rows_here = lax.psum_scatter(
            jnp.dot(leftover, sketch, preferred_element_type=jnp.float32),
            "col",
            scatter_dimension=0,
            tiled=True,
        )
        gram = lax.psum(local_gram(rows_here), ("row", "col")) / M
        outputs.append(make_basis(rows_here, gram))
    return jnp.stack(outputs, axis=0)


def solution(mesh):
    return jax.shard_map(
        body,
        mesh=mesh,
        in_specs=(P(None, "row", "col"), P(None, "row", "col"), P("col", None)),
        out_specs=P(None, ("row", "col"), None),
        check_vma=False,
    )
```

profile of v0, /device:TPU:0, one launch (start us, length us, event | category | flops | bytes accessed | tf_op | source)
XLA Modules:
  0.0 662.9 jit_solution(512142858564148330)
XLA Ops:
  7.4 14.6 %fusion.74 = (bf16[1,3072,1536]{2,1,0:T(8,128)(2,1)}, bf16[1,3072,1536]{2,1,0:T(8,128)(2,1)}) fusion(bf16[2,3072,1536]{2,1,0:T(8,128)(2,1)} %param.6), kind=kLoop, calls=%fused_computation.149 | loop fusion | bytes 37748736 | tf_op jit(solution)/shard_map/slice | solution.py:36
  22.0 12.7 %copy.22 = bf16[1,3072,1536]{1,2,0:T(8,128)(2,1)} copy(bf16[1,3072,1536]{2,1,0:T(8,128)(2,1)} %get-tuple-element.45) | data formatting | bytes 18874368
  41.8 11.6 %fusion.2 = f32[3072,512]{1,0:T(8,128)} fusion(bf16[1536,512]{1,0:T(8,128)(2,1)S(1)} %copy-done, bf16[192,8,24,128]{3,2,1,0:T(8,128)(2,1)} %bitcast.142, bf16[1,3072,1536]{1,2,0:T(8,128)(2,1)S(1)} %copy-done.4), kind=kOutput, calls=%fused_computation.8 | convolution fusion | flops 4836556800 | bytes 26738688 | tf_op jit(solution)/shard_map/dot_general | solution.py:41
  54.0 12.8 %copy.24 = bf16[1,3072,1536]{1,2,0:T(8,128)(2,1)} copy(bf16[1,3072,1536]{2,1,0:T(8,128)(2,1)} %get-tuple-element.46) | data formatting | bytes 18874368
  74.0 12.1 %fusion = f32[3072,512]{1,0:T(8,128)} fusion(bf16[1536,512]{1,0:T(8,128)(2,1)S(1)} %copy-done, bf16[192,8,24,128]{3,2,1,0:T(8,128)(2,1)} %bitcast.143, bf16[1,3072,1536]{1,2,0:T(8,128)(2,1)S(1)} %copy-done.5), kind=kOutput, calls=%fused_computation.5 | convolution fusion | flops 4836556800 | bytes 26738688 | tf_op jit(solution)/shard_map/dot_general | solution.py:41
  86.4 40.2 %reduce-scatter.3.cloned.1.call-done = f32[768,512]{1,0:T(8,128)} async-done(((f32[3072,512]{1,0:T(8,128)}), f32[768,512]{1,0:T(8,128)}) %reduce-scatter.3.cloned.1.call-update) | async-done | bytes 1572880 | tf_op jit(solution)/shard_map/reduce_scatter | solution.py:40
  132.2 67.6 %reduce-scatter.5.cloned.1.call-done = f32[768,512]{1,0:T(8,128)} async-done(((f32[3072,512]{1,0:T(8,128)}), f32[768,512]{1,0:T(8,128)}) %reduce-scatter.5.cloned.1.call-update) | async-done | bytes 1572880 | tf_op jit(solution)/shard_map/reduce_scatter | solution.py:40
  205.3 134.2 %all-reduce.4.cloned.1.call-done = (f32[512,512]{0,1:T(8,128)}, f32[512,512]{0,1:T(8,128)}) async-done(((f32[512,512]{0,1:T(8,128)}, f32[512,512]{0,1:T(8,128)}), (f32[512,512]{0,1:T(8,128)}, f32[512,512]{0,1:T(8,128)})) %all-reduce.4.cloned.1.call-update) | async-done | bytes 2097168 | tf_op jit(solution)/shard_map/psum | solution.py:46
  344.7 11.7 %cholesky.286 = f32[128,128]{1,0:T(8,128)S(1)} custom-call(f32[128,128]{1,0:T(8,128)S(1)} %cholesky.426), custom_call_target="Cholesky" | custom-call | tf_op jit(solution)/shard_map/jit(cholesky)/cholesky | solution.py:12
  356.4 10.0 %custom-call.27 = f32[1,128,128]{1,2,0:T(8,128)S(1)} custom-call(f32[1,128,128]{2,1,0:T(8,128)S(1)} %get-tuple-element.56), custom_call_target="InvertDiagBlocksLowerTriangular" | custom-call | tf_op jit(solution)/shard_map/jit(cholesky)/cholesky | solution.py:12
  369.1 11.7 %cholesky.305 = f32[128,128]{1,0:T(8,128)S(1)} custom-call(f32[128,128]{1,0:T(8,128)S(1)} %cholesky.430), custom_call_target="Cholesky" | custom-call | tf_op jit(solution)/shard_map/jit(cholesky)/cholesky | solution.py:12
  393.6 11.7 %cholesky.326 = f32[128,128]{1,0:T(8,128)S(1)} custom-call(f32[128,128]{1,0:T(8,128)S(1)} %cholesky.435), custom_call_target="Cholesky" | custom-call | tf_op jit(solution)/shard_map/jit(cholesky)/cholesky | solution.py:12
  406.1 10.2 %custom-call.29 = f32[1,128,128]{1,2,0:T(8,128)S(1)} custom-call(f32[1,128,128]{2,1,0:T(8,128)S(1)} %get-tuple-element.50), custom_call_target="InvertDiagBlocksLowerTriangular" | custom-call | tf_op jit(solution)/shard_map/jit(cholesky)/cholesky | solution.py:12
  417.7 11.7 %cholesky.343 = f32[128,128]{1,0:T(8,128)S(1)} custom-call(f32[128,128]{1,0:T(8,128)S(1)} %convolution_subtract_fusion.11), custom_call_target="Cholesky" | custom-call | tf_op jit(solution)/shard_map/jit(cholesky)/cholesky | solution.py:12
  433.7 11.6 %while.4 = (s32[]{:T(128)}, f32[512,512]{1,0:T(8,128)}, s32[4,2]{0,1:T(2,128)S(1)}, f32[4,128,128]{2,1,0:T(8,128)S(1)}, s32[]{:T(128)}) while((s32[]{:T(128)}, f32[512,512]{1,0:T(8,128)}, s32[4,2]{0,1:T(2,128)S(1)}, f32[4,128,128]{2,1,0:T(8,128)S(1)}, s32[]{:T(128)}) %tuple.56), condition=%wide.while_cond, body=%wide.while_body.sunk | while | flops 2 | bytes 131181 | solution.py:13
  445.4 39.5 %custom-call.30 = f32[4,128,128]{1,2,0:T(8,128)S(1)} custom-call(f32[4,128,128]{2,1,0:T(8,128)S(1)} %get-tuple-element.21), custom_call_target="InvertDiagBlocksLowerTriangular" | custom-call | tf_op jit(solution)/shard_map/triangular_solve/custom-call.3 | solution.py:13
  499.5 11.7 %cholesky.358 = f32[128,128]{1,0:T(8,128)S(1)} custom-call(f32[128,128]{1,0:T(8,128)S(1)} %cholesky.439), custom_call_target="Cholesky" | custom-call | tf_op jit(solution)/shard_map/jit(cholesky)/cholesky | solution.py:12
  511.3 10.0 %custom-call.31 = f32[1,128,128]{1,2,0:T(8,128)S(1)} custom-call(f32[1,128,128]{2,1,0:T(8,128)S(1)} %get-tuple-element.66), custom_call_target="InvertDiagBlocksLowerTriangular" | custom-call | tf_op jit(solution)/shard_map/jit(cholesky)/cholesky | solution.py:12
  523.9 11.7 %cholesky.377 = f32[128,128]{1,0:T(8,128)S(1)} custom-call(f32[128,128]{1,0:T(8,128)S(1)} %cholesky.443), custom_call_target="Cholesky" | custom-call | tf_op jit(solution)/shard_map/jit(cholesky)/cholesky | solution.py:12
  548.4 11.7 %cholesky.398 = f32[128,128]{1,0:T(8,128)S(1)} custom-call(f32[128,128]{1,0:T(8,128)S(1)} %cholesky.448), custom_call_target="Cholesky" | custom-call | tf_op jit(solution)/shard_map/jit(cholesky)/cholesky | solution.py:12
  560.9 10.2 %custom-call.33 = f32[1,128,128]{1,2,0:T(8,128)S(1)} custom-call(f32[1,128,128]{2,1,0:T(8,128)S(1)} %get-tuple-element.60), custom_call_target="InvertDiagBlocksLowerTriangular" | custom-call | tf_op jit(solution)/shard_map/jit(cholesky)/cholesky | solution.py:12
  572.5 11.7 %cholesky.415 = f32[128,128]{1,0:T(8,128)S(1)} custom-call(f32[128,128]{1,0:T(8,128)S(1)} %convolution_subtract_fusion.10), custom_call_target="Cholesky" | custom-call | tf_op jit(solution)/shard_map/jit(cholesky)/cholesky | solution.py:12
  588.7 11.7 %while.5 = (s32[]{:T(128)}, f32[512,512]{1,0:T(8,128)}, s32[4,2]{0,1:T(2,128)S(1)}, f32[4,128,128]{2,1,0:T(8,128)S(1)}, s32[]{:T(128)}) while((s32[]{:T(128)}, f32[512,512]{1,0:T(8,128)}, s32[4,2]{0,1:T(2,128)S(1)}, f32[4,128,128]{2,1,0:T(8,128)S(1)}, s32[]{:T(128)}) %tuple.66), condition=%wide.while_cond.clone, body=%wide.while_body.clone.sunk | while | flops 2 | bytes 131181 | solution.py:13
  600.4 39.5 %custom-call.34 = f32[4,128,128]{1,2,0:T(8,128)S(1)} custom-call(f32[4,128,128]{2,1,0:T(8,128)S(1)} %get-tuple-element.22), custom_call_target="InvertDiagBlocksLowerTriangular" | custom-call | tf_op jit(solution)/shard_map/triangular_solve/custom-call.3 | solution.py:13
  (126 shorter events, 125.1 us)
Async XLA Ops:
  6.5 34.2 %copy-start = (bf16[1536,512]{1,0:T(8,128)(2,1)S(1)}, bf16[1536,512]{1,0:T(8,128)(2,1)}, u32[]{:S(2)}) copy-start(bf16[1536,512]{1,0:T(8,128)(2,1)} %param.8) | copy-start | bytes 4718596
  6.5 120.0 %reduce-scatter.3.cloned.1.call-start = ((), (), s32[]{:S(2)}) async-start(), calls=%async_computation.2 | async-start | bytes 7864320 | tf_op jit(solution)/shard_map/reduce_scatter | solution.py:40
  34.7 7.1 %copy-start.4 = (bf16[1,3072,1536]{1,2,0:T(8,128)(2,1)S(1)}, bf16[1,3072,1536]{1,2,0:T(8,128)(2,1)}, u32[]{:S(2)}) copy-start(bf16[1,3072,1536]{1,2,0:T(8,128)(2,1)} %copy.22) | copy-start | bytes 28311556
  53.5 146.3 %reduce-scatter.5.cloned.1.call-start = ((), (), s32[]{:S(2)}) async-start(), calls=%async_computation.3 | async-start | bytes 7864320 | tf_op jit(solution)/shard_map/reduce_scatter | solution.py:40
  66.8 7.2 %copy-start.5 = (bf16[1,3072,1536]{1,2,0:T(8,128)(2,1)S(1)}, bf16[1,3072,1536]{1,2,0:T(8,128)(2,1)}, u32[]{:S(2)}) copy-start(bf16[1,3072,1536]{1,2,0:T(8,128)(2,1)} %copy.24) | copy-start | bytes 28311556
  86.2 253.3 %all-reduce.4.cloned.1.call-start = ((), (), s32[]{:S(2)}) async-start(), calls=%async_computation.4 | async-start | bytes 4194304 | tf_op jit(solution)/shard_map/psum | solution.py:46
  341.8 1.7 copy-start.8
  343.7 1.0 copy-start.9
  432.6 52.3 %copy-start.3 = (f32[768,512]{1,0:T(8,128)S(1)}, f32[768,512]{1,0:T(8,128)}, u32[]{:S(2)}) copy-start(f32[768,512]{1,0:T(8,128)} %reduce-scatter.3.cloned.1.call-done) | copy-start | bytes 4718596
  494.0 1.6 copy-start.7
  498.5 1.0 copy-start.10
  587.5 52.4 %copy-start.2 = (f32[768,512]{1,0:T(8,128)S(1)}, f32[768,512]{1,0:T(8,128)}, u32[]{:S(2)}) copy-start(f32[768,512]{1,0:T(8,128)} %reduce-scatter.5.cloned.1.call-done) | copy-start | bytes 4718596
  649.1 1.4 copy-start.6
  652.5 3.7 copy-start.1
Sparse Core Ops, SparseCore 0:
  53.6 72.9 reduce-scatter.2
  129.5 70.1 reduce-scatter.4
  205.5 134.0 all-reduce.3
where the time goes:
time: 670 us; the launch traced here: 663 us
  other arithmetic  248 us (37%)
  waiting for transfers between devices  242 us (36%)
  local copies, waits for them, and re-layouts  89.1 us (13%)
  matrix products  64.1 us (10%)
  between operations  18.9 us (3%)
    another operation x30, other arithmetic, make_basis(): lower = jnp.linalg.cholesky(gram)  159 us
    psum x1, waiting for transfers between devices, body(): gram = lax.psum(local_gram(rows_here), ('row', 'col')) / M  134 us
    reduce_scatter x2, waiting for transfers between devices, body(): lax.psum_scatter(jnp.dot(leftover, sketch, preferred_element_type=jnp.flo...  108 us
    another operation x5, other arithmetic, make_basis(): lax.linalg.triangular_solve(lower, rows_here, left_side=False, lower=True...  81.2 us
    unnamed x24, local copies, waits for them, and re-layouts  31 us
    dot_general x2, matrix products, body(): jnp.dot(leftover, sketch, preferred_element_type=jnp.float32)  23.8 us
    another operation x27, local copies, waits for them, and re-layouts, make_basis(): lax.linalg.triangular_solve(lower, rows_here, left_side=False, lower=True...  23.2 us
    another operation x14, matrix products, make_basis(): lax.linalg.triangular_solve(lower, rows_here, left_side=False, lower=True...  18.2 us
  transfers between devices with their start and end apart: 3, of which 3 were waited for; matrix products, arithmetic and copies ran while one was open for 6% of the time, Pallas kernels for 0%

commit v1 on v0

v1 whole, which is shorter than its diff:
```python
import jax
import jax.numpy as jnp
from jax import lax
from jax.experimental import pallas as pl
from jax.experimental.pallas import tpu as pltpu
from jax.sharding import PartitionSpec as P

BLOCK = 128
LAYERS = 2
GROUP = 8


def split(x):
    high = x.astype(jnp.bfloat16)
    low = (x - high.astype(jnp.float32)).astype(jnp.bfloat16)
    return high, low


def dot3(a, b, dims):
    a_high, a_low = split(a)
    b_high, b_low = split(b)

    def one(x, y):
        return lax.dot_general(x, y, (dims, ((), ())), preferred_element_type=jnp.float32)

    return one(a_high, b_high) + (one(a_high, b_low) + one(a_low, b_high))


def sample_kernel(keep_ref, w_ref, s_ref, o_ref):
    rows = w_ref.shape[1]
    parts = []
    for block in range(rows // BLOCK):
        parts.append(w_ref[0, block * BLOCK : (block + 1) * BLOCK, :] * keep_ref[0, block])
    leftover = jnp.concatenate(parts, axis=0)
    o_ref[...] = jnp.dot(leftover, s_ref[...], preferred_element_type=jnp.float32)


def sample(weights, keep, sketch, layer):
    _, row_count, col_count = weights.shape
    width = sketch.shape[1]
    tile = min(512, row_count)
    while row_count % tile:
        tile -= BLOCK
    return pl.pallas_call(
        sample_kernel,
        grid=(row_count // tile,),
        in_specs=[
            pl.BlockSpec((1, tile // BLOCK, 1, col_count), lambda i: (layer, i, 0, 0)),
            pl.BlockSpec((1, tile, col_count), lambda i: (layer, i, 0)),
            pl.BlockSpec((col_count, width), lambda i: (0, 0)),
        ],
        out_specs=pl.BlockSpec((tile, width), lambda i: (i, 0)),
        out_shape=jax.ShapeDtypeStruct((row_count, width), jnp.float32),
        compiler_params=pltpu.CompilerParams(vmem_limit_bytes=40 * 2**20),
        cost_estimate=pl.CostEstimate(
            flops=2 * row_count * col_count * width,
            bytes_accessed=2 * row_count * col_count + 4 * row_count * width,
            transcendentals=0,
        ),
        name="sample",
    )(keep, weights, sketch)


def factor_block(d, size):
    row = lax.broadcasted_iota(jnp.int32, (size, size), 0)
    col = lax.broadcasted_iota(jnp.int32, (size, size), 1)
    e = (row == col).astype(jnp.float32)
    sub = lax.broadcasted_iota(jnp.int32, (GROUP, size), 0)
    done = []
    for start in range(0, size, GROUP):
        live = size - start
        cols = [
            jnp.broadcast_to(d[:, start + k : start + k + 1], (live, size)) for k in range(GROUP)
        ]
        head_cols = [c[:GROUP] for c in cols]
        tail_cols = [c[GROUP:] for c in cols]
        head_d, tail_d = d[:GROUP], d[GROUP:]
        head_e, tail_e = e[:GROUP], e[GROUP:]
        scale = jnp.zeros((GROUP, size), jnp.float32)
        for k in range(GROUP):
            pivot = head_cols[k][k : k + 1]
            inverse = 1.0 / pivot
            scale = jnp.where(sub == k, lax.rsqrt(pivot), scale)
            factor = jnp.where(sub > k, head_cols[k], 0.0)
            row_e = head_e[k : k + 1] * inverse
            row_d = head_d[k : k + 1] * inverse
            for j in range(k + 1, GROUP):
                step = head_cols[j][k : k + 1] * inverse
                head_cols[j] = head_cols[j] - factor * step
                if live > GROUP:
                    tail_cols[j] = tail_cols[j] - tail_cols[k] * step
            head_d = head_d - factor * row_d
            head_e = head_e - factor * row_e
            if live > GROUP:
                tail_d = tail_d - tail_cols[k] * row_d
                tail_e = tail_e - tail_cols[k] * row_e
        done.append(head_e * scale)
        d, e = tail_d, tail_e
    return jnp.concatenate(done, axis=0)


def inverse_kernel(total_rows, g_ref, o_ref, a, x):
    width = g_ref.shape[0]
    count = width // BLOCK
    a[...] = g_ref[...]
    x[...] = jnp.zeros_like(x)

    @pl.loop(0, count)
    def _(k):
        here = pl.ds(pl.multiple_of(k * BLOCK, BLOCK), BLOCK)
        inner = factor_block(a[here, here], BLOCK)
        for now in range(count):

            @pl.when(k == now)
            def _():
                lo, hi = now * BLOCK, (now + 1) * BLOCK
                if now:
                    mine = dot3(inner, x[lo:hi, :lo], ((1,), (0,)))
                    x[lo:hi, :lo] = mine
                x[lo:hi, lo:hi] = inner
                if now < count - 1:
                    right = dot3(inner, a[lo:hi, hi:], ((1,), (0,)))
                    a[hi:, hi:] -= dot3(right, right, ((0,), (0,)))
                    x[hi:, :hi] -= dot3(right, x[lo:hi, :hi], ((0,), (0,)))

    o_ref[...] = x[...].T * jnp.float32(total_rows)


def invert(g, total_rows):
    width = g.shape[0]
    return pl.pallas_call(
        lambda *refs: inverse_kernel(total_rows, *refs),
        in_specs=[pl.BlockSpec(memory_space=pltpu.VMEM)],
        out_specs=pl.BlockSpec(memory_space=pltpu.VMEM),
        out_shape=jax.ShapeDtypeStruct((width, width), jnp.float32),
        scratch_shapes=[pltpu.VMEM((width, width), jnp.float32)] * 2,
        compiler_params=pltpu.CompilerParams(vmem_limit_bytes=40 * 2**20),
        cost_estimate=pl.CostEstimate(
            flops=40 * 10**9, bytes_accessed=8 * width * width, transcendentals=0
        ),
        name="invert",
    )(g)


def apply_kernel(r_ref, u_ref, *rest):
    rest[-1][0] = dot3(r_ref[...], u_ref[...], ((1,), (0,)))


def apply(rows_here, upper, layer, out):
    row_count, width = rows_here.shape
    tile = min(256, row_count)
    while row_count % tile:
        tile -= 8
    extra = [] if out is None else [pl.BlockSpec(memory_space=pl.ANY)]
    return pl.pallas_call(
        apply_kernel,
        grid=(row_count // tile,),
        in_specs=[
            pl.BlockSpec((tile, width), lambda i: (i, 0)),
            pl.BlockSpec((width, width), lambda i: (0, 0)),
        ]
        + extra,
        out_specs=pl.BlockSpec((1, tile, width), lambda i: (layer, i, 0)),
        out_shape=jax.ShapeDtypeStruct((LAYERS, row_count, width), jnp.float32),
        input_output_aliases={} if out is None else {2: 0},
        compiler_params=pltpu.CompilerParams(vmem_limit_bytes=40 * 2**20),
        cost_estimate=pl.CostEstimate(
            flops=6 * row_count * width * width,
            bytes_accessed=8 * row_count * width,
            transcendentals=0,
        ),
        name="apply",
    )(rows_here, upper, *([] if out is None else [out]))


def local_gram(rows_here):
    return lax.dot_general(
        rows_here,
        rows_here,
        (((0,), (0,)), ((), ())),
        precision=lax.Precision.HIGH,
        preferred_element_type=jnp.float32,
    )


def make_body(total_shards):
    def body(weights, pattern, sketch):
        total_rows = weights.shape[1] * total_shards
        keep = jnp.repeat((1 - pattern).astype(jnp.bfloat16), BLOCK, axis=2)[:, :, None, :]
        rows = []
        for layer in range(LAYERS):
            part = sample(weights, keep, sketch, layer)
            rows.append(lax.psum_scatter(part, "col", scatter_dimension=0, tiled=True))
        out = None
        for layer in range(LAYERS):
            gram = lax.psum(local_gram(rows[layer]), ("row", "col"))
            out = apply(rows[layer], invert(gram, total_rows), layer, out)
        return out

    return body


def solution(mesh):
    return jax.shard_map(
        make_body(mesh.shape["row"]),
        mesh=mesh,
        in_specs=(P(None, "row", "col"), P(None, "row", "col"), P("col", None)),
        out_specs=P(None, ("row", "col"), None),
        check_vma=False,
    )
```

time: 670 us -> 352 us (0.53)
  other arithmetic: 248 us -> 0.71 us
  local copies, waits for them, and re-layouts: 89.1 us -> 9.63 us
  matrix products: 64.1 us -> 8.63 us
  Pallas kernels: 0 us -> 54.4 us
  waiting for transfers between devices: 242 us -> 265 us
    another operation x38 -> x0, other arithmetic: 244 us -> none  [the longest x30 159 us: make_basis(): lower = jnp.linalg.cholesky(gram)]
    pallas_call x0 -> x6, Pallas kernels: none -> 54.4 us  [the longest x2 32.1 us: invert(): pl.pallas_call(lambda *refs: inverse_kernel(total_rows, *refs), in_specs=...]
    another operation x26 -> x0, matrix products: 29.2 us -> none  [the longest x14 18.2 us: make_basis(): lax.linalg.triangular_solve(lower, rows_here, left_side=False, lower=True...]
    another operation x36 -> x1, local copies, waits for them, and re-layouts: 27.2 us -> 0.08 us  [body(): jnp.repeat((1 - pattern).astype(jnp.bfloat16), BLOCK, axis=2)[:, :, None, :]]
    dot_general x2 -> x0, matrix products: 23.8 us -> none  [body(): jnp.dot(leftover, sketch, preferred_element_type=jnp.float32)]
    unnamed x24 -> x16, local copies, waits for them, and re-layouts: 31 us -> 9.28 us
    reduce_scatter x2, waiting for transfers between devices: 108 us -> 129 us  [body(): rows.append(lax.psum_scatter(part, 'col', scatter_dimension=0, tiled=True))]
    slice x2 -> x0, local copies, waits for them, and re-layouts: 15.5 us -> none  [the longest x1 14.6 us: body(): weights[layer].reshape(row_count // BLOCK, BLOCK, col_count // BLOCK, BLOCK)]
  transfers between devices with their start and end apart: 3 -> 3, of which waited for: 3 -> 3; matrix products, arithmetic and copies ran while one was open for 6% -> 1% of each run, Pallas kernels for 0% -> 2%
where the time goes in v1:
time: 352 us; the launch traced here: 351 us
  waiting for transfers between devices  265 us (75%)
  Pallas kernels  54.4 us (15%)
  between operations  13.2 us (4%)
  local copies, waits for them, and re-layouts  9.63 us (3%)
  matrix products  8.63 us (2%)
    psum x1, waiting for transfers between devices, body(): gram = lax.psum(local_gram(rows[layer]), ('row', 'col'))  135 us
    reduce_scatter x2, waiting for transfers between devices, body(): rows.append(lax.psum_scatter(part, 'col', scatter_dimension=0, tiled=True))  129 us
    pallas_call x2, Pallas kernels, invert(): pl.pallas_call(lambda *refs: inverse_kernel(total_rows, *refs), in_specs=...  32.1 us
    pallas_call x2, Pallas kernels, sample(): pl.pallas_call(sample_kernel, grid=(row_count // tile,), in_specs=[pl.Blo...  16.8 us
    unnamed x16, local copies, waits for them, and re-layouts  9.28 us
    dot_general x2, matrix products, local_gram(): lax.dot_general(rows_here, rows_here, (((0,), (0,)), ((), ())), precision...  8.63 us
  transfers between devices with their start and end apart: 3, of which 3 were waited for; matrix products, arithmetic and copies ran while one was open for 1% of the time, Pallas kernels for 2%

profile of v1, /device:TPU:0, one launch (start us, length us, event | category | flops | bytes accessed | tf_op | source)
XLA Modules:
  0.0 351.4 jit_solution(7889223201038206066)
XLA Ops:
  6.5 0.7 subtract_convert_fusion
  7.3 0.1 copy.6
  7.4 0.2 broadcast_in_dim.3
  7.5 0.1 broadcast_in_dim_reshape.4.keep_ref
  7.6 1.4 copy-done.4
  9.0 8.4 %sample.3 = f32[3072,512]{1,0:T(8,128)S(1)} custom-call(bf16[2,24,1,1536]{3,2,1,0:T(2,128)(2,1)S(1)} %broadcast_in_dim_reshape.4.keep_ref, bf16[2,3072,1536]{2,1,0:T(8,128)(2,1)} %w_ref.3, bf16[1536,512]{1,0:T(8,128)(2,1)S(1)} %copy-done.4), custom_call_target="tpu_custom_call" | custom-call | flops 4831838208 | bytes 15728640 | tf_op jit(solution)/shard_map/sample/pallas_call | solution.py:44
  17.4 2.6 copy-done
  20.1 0.0 reduce-scatter.3.cloned.1.call-start
  20.1 1.3 copy-done.5
  21.5 8.4 %sample.2 = f32[3072,512]{1,0:T(8,128)S(1)} custom-call(bf16[2,24,1,1536]{3,2,1,0:T(2,128)(2,1)S(1)} %broadcast_in_dim_reshape.4.keep_ref, bf16[2,3072,1536]{2,1,0:T(8,128)(2,1)} %w_ref.3, bf16[1536,512]{1,0:T(8,128)(2,1)S(1)} %copy-done.5), custom_call_target="tpu_custom_call" | custom-call | flops 4831838208 | bytes 15728640 | tf_op jit(solution)/shard_map/sample/pallas_call | solution.py:44
  29.9 2.7 copy-done.1
  32.5 0.0 reduce-scatter.3.cloned.1.call-update
  32.6 0.0 all-reduce.3.cloned.1.call-start
  32.6 60.6 %reduce-scatter.5.cloned.1.call-done.r_ref = f32[768,512]{1,0:T(8,128)} async-done(((f32[3072,512]{1,0:T(8,128)}), f32[768,512]{1,0:T(8,128)}) %reduce-scatter.5.cloned.1.call-update) | async-done | bytes 1572880 | tf_op jit(solution)/shard_map/reduce_scatter | solution.py:193
  93.2 4.4 %fusion.1 = f32[512,512]{1,0:T(8,128)} fusion(f32[768,512]{1,0:T(8,128)} %reduce-scatter.5.cloned.1.call-done.r_ref), kind=kOutput, calls=%fused_computation.2 | convolution fusion | flops 1207959552 | bytes 2621440 | tf_op jit(solution)/shard_map/dot_general | solution.py:177
  97.5 68.8 %reduce-scatter.3.cloned.1.call-done.r_ref = f32[768,512]{1,0:T(8,128)} async-done(((f32[3072,512]{1,0:T(8,128)}), f32[768,512]{1,0:T(8,128)}) %reduce-scatter.3.cloned.1.call-update) | async-done | bytes 1572880 | tf_op jit(solution)/shard_map/reduce_scatter | solution.py:193
  166.4 4.3 %fusion = f32[512,512]{1,0:T(8,128)} fusion(f32[768,512]{1,0:T(8,128)} %reduce-scatter.3.cloned.1.call-done.r_ref), kind=kOutput, calls=%fused_computation.1 | convolution fusion | flops 1207959552 | bytes 2621440 | tf_op jit(solution)/shard_map/dot_general | solution.py:177
  170.7 0.0 all-reduce.3.cloned.1.call-update
  170.7 135.2 %all-reduce.3.cloned.1.call-done = (f32[512,512]{1,0:T(8,128)}, f32[512,512]{1,0:T(8,128)}) async-done(((f32[512,512]{1,0:T(8,128)}, f32[512,512]{1,0:T(8,128)}), (f32[512,512]{1,0:T(8,128)}, f32[512,512]{1,0:T(8,128)})) %all-reduce.3.cloned.1.call-update) | async-done | bytes 2097168 | tf_op jit(solution)/shard_map/psum | solution.py:196
  305.9 1.2 copy-done.7
  307.2 16.1 %invert.2.u_ref = f32[512,512]{1,0:T(8,128)S(1)} custom-call(f32[512,512]{1,0:T(8,128)S(1)} %copy-done.7), custom_call_target="tpu_custom_call" | custom-call | flops 40000000000 | bytes 2097152 | tf_op jit(solution)/shard_map/invert/pallas_call | solution.py:131
  323.3 15.9 %invert.3.u_ref = f32[512,512]{1,0:T(8,128)S(1)} custom-call(f32[512,512]{1,0:T(8,128)S(1)} %copy-done.6), custom_call_target="tpu_custom_call" | custom-call | flops 40000000000 | bytes 2097152 | tf_op jit(solution)/shard_map/invert/pallas_call | solution.py:131
  339.3 2.8 apply.2.rest_0_
  342.1 2.8 apply.3
  (13 shorter events, 0.0 us)
Async XLA Ops:
  6.5 86.6 %reduce-scatter.5.cloned.1.call-start = ((), (), s32[]{:S(2)}) async-start(), calls=%async_computation.3 | async-start | bytes 7864320 | tf_op jit(solution)/shard_map/reduce_scatter | solution.py:193
  7.6 1.4 copy-start.4
  17.4 2.7 copy-start
  20.1 1.4 copy-start.5
  20.1 146.3 %reduce-scatter.3.cloned.1.call-start = ((), (), s32[]{:S(2)}) async-start(), calls=%async_computation.2 | async-start | bytes 7864320 | tf_op jit(solution)/shard_map/reduce_scatter | solution.py:193
  29.9 2.7 copy-start.1
  32.6 273.4 %all-reduce.3.cloned.1.call-start = ((), (), s32[]{:S(2)}) async-start(), calls=%async_computation.4 | async-start | bytes 4194304 | tf_op jit(solution)/shard_map/psum | solution.py:196
  305.9 1.2 copy-start.7
  307.1 16.1 %copy-start.6 = (f32[512,512]{1,0:T(8,128)S(1)}, f32[512,512]{1,0:T(8,128)}, u32[]{:S(2)}) copy-start(f32[512,512]{1,0:T(8,128)} %get-tuple-element.6.refs_0_) | copy-start | bytes 3145732
  323.3 16.0 %copy-start.2 = (f32[768,512]{1,0:T(8,128)S(1)}, f32[768,512]{1,0:T(8,128)}, u32[]{:S(2)}) copy-start(f32[768,512]{1,0:T(8,128)} %reduce-scatter.5.cloned.1.call-done.r_ref) | copy-start | bytes 4718596
  339.3 2.8 copy-start.3
Sparse Core Ops, SparseCore 0:
  20.2 72.9 reduce-scatter.4
  96.2 70.1 reduce-scatter.2
  171.9 133.9 all-reduce.2

commit v2 on v1

v2 whole, which is shorter than its diff:
```python
import jax
import jax.numpy as jnp
from jax import lax
from jax.experimental import pallas as pl
from jax.experimental.pallas import tpu as pltpu
from jax.sharding import PartitionSpec as P

BLOCK = 128
LAYERS = 2
GROUP = 8


def split(x):
    high = x.astype(jnp.bfloat16)
    low = (x - high.astype(jnp.float32)).astype(jnp.bfloat16)
    return high, low


def dot3(a, b, dims):
    a_high, a_low = split(a)
    b_high, b_low = split(b)

    def one(x, y):
        return lax.dot_general(x, y, (dims, ((), ())), preferred_element_type=jnp.float32)

    return one(a_high, b_high) + (one(a_high, b_low) + one(a_low, b_high))


def sample_kernel(keep_ref, w_ref, s_ref, o_ref):
    rows = w_ref.shape[1]
    parts = []
    for block in range(rows // BLOCK):
        parts.append(w_ref[0, block * BLOCK : (block + 1) * BLOCK, :] * keep_ref[0, block])
    leftover = jnp.concatenate(parts, axis=0)
    o_ref[...] = jnp.dot(leftover, s_ref[...], preferred_element_type=jnp.float32)


def sample(weights, keep, sketch, layer):
    _, row_count, col_count = weights.shape
    width = sketch.shape[1]
    tile = min(512, row_count)
    while row_count % tile:
        tile -= BLOCK
    return pl.pallas_call(
        sample_kernel,
        grid=(row_count // tile,),
        in_specs=[
            pl.BlockSpec((1, tile // BLOCK, 1, col_count), lambda i: (layer, i, 0, 0)),
            pl.BlockSpec((1, tile, col_count), lambda i: (layer, i, 0)),
            pl.BlockSpec((col_count, width), lambda i: (0, 0)),
        ],
        out_specs=pl.BlockSpec((tile, width), lambda i: (i, 0)),
        out_shape=jax.ShapeDtypeStruct((row_count, width), jnp.float32),
        compiler_params=pltpu.CompilerParams(vmem_limit_bytes=40 * 2**20),
        cost_estimate=pl.CostEstimate(
            flops=2 * row_count * col_count * width,
            bytes_accessed=2 * row_count * col_count + 4 * row_count * width,
            transcendentals=0,
        ),
        name="sample",
    )(keep, weights, sketch)


def factor_blocks(blocks, size):
    many = range(len(blocks))
    row = lax.broadcasted_iota(jnp.int32, (size, size), 0)
    col = lax.broadcasted_iota(jnp.int32, (size, size), 1)
    eye = (row == col).astype(jnp.float32)
    sub = lax.broadcasted_iota(jnp.int32, (GROUP, size), 0)
    d = list(blocks)
    e = [eye for _ in many]
    done = [[] for _ in many]
    for start in range(0, size, GROUP):
        live = size - start
        cols = [
            [
                jnp.broadcast_to(d[n][:, start + k : start + k + 1], (live, size))
                for k in range(GROUP)
            ]
            for n in many
        ]
        head_cols = [[c[:GROUP] for c in cols[n]] for n in many]
        tail_cols = [[c[GROUP:] for c in cols[n]] for n in many]
        head_d, tail_d = [x[:GROUP] for x in d], [x[GROUP:] for x in d]
        head_e, tail_e = [x[:GROUP] for x in e], [x[GROUP:] for x in e]
        scale = [jnp.zeros((GROUP, size), jnp.float32) for _ in many]
        for k in range(GROUP):
            for n in many:
                pivot = head_cols[n][k][k : k + 1]
                inverse = 1.0 / pivot
                scale[n] = jnp.where(sub == k, lax.rsqrt(pivot), scale[n])
                factor = jnp.where(sub > k, head_cols[n][k], 0.0)
                row_e = head_e[n][k : k + 1] * inverse
                row_d = head_d[n][k : k + 1] * inverse
                for j in range(k + 1, GROUP):
                    step = head_cols[n][j][k : k + 1] * inverse
                    head_cols[n][j] = head_cols[n][j] - factor * step
                    if live > GROUP:
                        tail_cols[n][j] = tail_cols[n][j] - tail_cols[n][k] * step
                head_d[n] = head_d[n] - factor * row_d
                head_e[n] = head_e[n] - factor * row_e
                if live > GROUP:
                    tail_d[n] = tail_d[n] - tail_cols[n][k] * row_d
                    tail_e[n] = tail_e[n] - tail_cols[n][k] * row_e
        for n in many:
            done[n].append(head_e[n] * scale[n])
        d, e = tail_d, tail_e
    return [jnp.concatenate(done[n], axis=0) for n in many]


def upper_blocks(width):
    count = width // BLOCK
    return [(i, j) for i in range(count) for j in range(i, count)]


def inverse_kernel(total_rows, g_ref, o_ref, a, x):
    layers, width = a.shape[0], a.shape[1]
    count = width // BLOCK
    a[...] = jnp.zeros_like(a)
    x[...] = jnp.zeros_like(x)
    for b, (i, j) in enumerate(upper_blocks(width)):
        for n in range(layers):
            a[n, i * BLOCK : (i + 1) * BLOCK, j * BLOCK : (j + 1) * BLOCK] = g_ref[
                n, b * BLOCK : (b + 1) * BLOCK
            ]

    @pl.loop(0, count)
    def _(k):
        here = pl.ds(pl.multiple_of(k * BLOCK, BLOCK), BLOCK)
        inners = factor_blocks([a[n, here, here] for n in range(layers)], BLOCK)
        for now in range(count):

            @pl.when(k == now)
            def _():
                lo, hi = now * BLOCK, (now + 1) * BLOCK
                for n in range(layers):
                    if now:
                        x[n, lo:hi, :lo] = dot3(inners[n], x[n, lo:hi, :lo], ((1,), (0,)))
                    x[n, lo:hi, lo:hi] = inners[n]
                    if now < count - 1:
                        right = dot3(inners[n], a[n, lo:hi, hi:], ((1,), (0,)))
                        a[n, hi:, hi:] -= dot3(right, right, ((0,), (0,)))
                        x[n, hi:, :hi] -= dot3(right, x[n, lo:hi, :hi], ((0,), (0,)))

    for n in range(layers):
        o_ref[n] = x[n].T * jnp.float32(total_rows)


def invert(g, width, total_rows):
    layers = g.shape[0]
    return pl.pallas_call(
        lambda *refs: inverse_kernel(total_rows, *refs),
        in_specs=[pl.BlockSpec(memory_space=pltpu.VMEM)],
        out_specs=pl.BlockSpec(memory_space=pltpu.VMEM),
        out_shape=jax.ShapeDtypeStruct((layers, width, width), jnp.float32),
        scratch_shapes=[pltpu.VMEM((layers, width, width), jnp.float32)] * 2,
        compiler_params=pltpu.CompilerParams(vmem_limit_bytes=40 * 2**20),
        cost_estimate=pl.CostEstimate(
            flops=40 * 10**9, bytes_accessed=8 * width * width, transcendentals=0
        ),
        name="invert",
    )(g)


def apply_kernel(r_ref, u_ref, o_ref):
    o_ref[0] = dot3(r_ref[0], u_ref[0], ((1,), (0,)))


def apply(rows_here, upper):
    layers, row_count, width = rows_here.shape
    tile = min(256, row_count)
    while row_count % tile:
        tile -= 8
    return pl.pallas_call(
        apply_kernel,
        grid=(layers, row_count // tile),
        in_specs=[
            pl.BlockSpec((1, tile, width), lambda l, i: (l, i, 0)),
            pl.BlockSpec((1, width, width), lambda l, i: (l, 0, 0)),
        ],
        out_specs=pl.BlockSpec((1, tile, width), lambda l, i: (l, i, 0)),
        out_shape=jax.ShapeDtypeStruct((layers, row_count, width), jnp.float32),
        compiler_params=pltpu.CompilerParams(vmem_limit_bytes=40 * 2**20),
        cost_estimate=pl.CostEstimate(
            flops=6 * layers * row_count * width * width,
            bytes_accessed=8 * layers * row_count * width,
            transcendentals=0,
        ),
        name="apply",
    )(rows_here, upper)


MESH = pl.DeviceIdType.MESH


def remote(src, dst, send, recv, device):
    return pltpu.make_async_remote_copy(
        src_ref=src, dst_ref=dst, send_sem=send, recv_sem=recv, device_id=device, device_id_type=MESH
    )


def fused_kernel(
    cols, chips, keep_ref, w_ref, s_ref, rows_ref, g_ref,
    wbuf, part, inbox, pack, pair, box, full,
    wsem, rs_send, rs_recv, pair_send, pair_recv, out_send, out_recv, all_send, all_recv,
    back_send, back_recv,
):
    row, col = lax.axis_index("row"), lax.axis_index("col")
    core, z = row % 2, row // 2
    cx, cy = col % 2, col // 2
    me = z * cols + col
    half = wbuf.shape[1]
    width = s_ref.shape[1]
    blocks = half // BLOCK
    share = pack.shape[1] // 2
    piece = share // chips
    to_x = (row, cy * 2 + (1 - cx))
    to_y = (row, (1 - cy) * 2 + cx)
    partner = (row + 1 - 2 * core, col)

    def peer(offset):
        p = (me + offset) % chips
        return p, ((p // cols) * 2 + core, p % cols)

    barrier = pltpu.get_barrier_semaphore()
    pl.semaphore_signal(barrier, inc=1, device_id=partner, device_id_type=MESH)
    for offset in range(1, chips):
        pl.semaphore_signal(barrier, inc=1, device_id=peer(offset)[1], device_id_type=MESH)

    slots = [(1, 1, 0), (1, 1, 1), (1, 0, 0), (0, 1, 1), (0, 1, 0), (1, 0, 1), (0, 0, 0), (0, 0, 1)]

    def first_block(slot):
        dx, dy, part_of = slots[slot]
        owner = ((cy + dy) % 2) * 2 + (cx + dx) % 2
        return (owner * 2 + part_of) * blocks

    def fetch(step):
        layer, slot = step // 8, step % 8
        start = pl.multiple_of(first_block(slot) * BLOCK, BLOCK)
        return pltpu.make_async_copy(
            w_ref.at[layer, pl.ds(start, half)], wbuf.at[step % 2], wsem.at[step % 2]
        )

    def product(step):
        layer, slot = step // 8, step % 8
        if step + 1 < 8 * LAYERS:
            fetch(step + 1).start()
        fetch(step).wait()
        first = first_block(slot)
        kept = [
            wbuf[step % 2, b * BLOCK : (b + 1) * BLOCK, :] * keep_ref[layer, first + b]
            for b in range(blocks)
        ]
        part[layer, slot] = jnp.dot(
            jnp.concatenate(kept, axis=0), s_ref[...], preferred_element_type=jnp.float32
        )

    targets = [to_x, to_y, to_x, to_y, to_y, to_x]

    def hop(layer, k):
        return remote(
            part.at[layer, k], inbox.at[layer, k],
            rs_send.at[layer, k], rs_recv.at[layer, k], targets[k],
        )

    def combine(layer):
        for k in (0, 1):
            hop(layer, k).wait_recv()
            part[layer, 4 + k] += inbox[layer, k]
            hop(layer, 4 + k).start()

    def gather_rows(layer):
        for k in (0, 1):
            hop(layer, 2 + k).wait_recv()
            hop(layer, 4 + k).wait_recv()
            rows_ref[layer, k * half : (k + 1) * half] = (
                part[layer, 6 + k] + inbox[layer, 2 + k] + inbox[layer, 4 + k]
            )

    def gram(layer):
        at = 0
        for i in range(width // BLOCK):
            lo = i * BLOCK
            g = dot3(
                rows_ref[layer, :, lo : lo + BLOCK], rows_ref[layer, :, lo:], ((0,), (0,))
            )
            for j in range((width - lo) // BLOCK):
                pack[layer, at : at + BLOCK] = g[:, j * BLOCK : (j + 1) * BLOCK]
                at += BLOCK

    def pair_copy(layer):
        other = pl.ds(pl.multiple_of((1 - core) * share, 8), share)
        return remote(
            pack.at[layer, other], pair.at[layer],
            pair_send.at[layer], pair_recv.at[layer], partner,
        )

    def out_copy(layer, offset):
        p, device = peer(offset)
        mine = pl.ds(pl.multiple_of(core * share + p * piece, 8), piece)
        return remote(
            pack.at[layer, mine], box.at[layer, offset],
            out_send.at[layer, offset], out_recv.at[layer, offset], device,
        )

    def all_copy(layer, offset):
        device = peer(offset)[1]
        here = full.at[layer, core, pl.ds(pl.multiple_of(me * piece, 8), piece)]
        return remote(
            here, here, all_send.at[layer, offset], all_recv.at[layer, offset], device
        )

    def back_copy(layer):
        here = full.at[layer, core]
        return remote(here, here, back_send.at[layer], back_recv.at[layer], partner)

    def sum_start(layer):
        pair_copy(layer).start()
        pair_copy(layer).wait_recv()
        own = pl.ds(pl.multiple_of(core * share, 8), share)
        pack[layer, own] += pair[layer]
        for offset in range(1, chips):
            out_copy(layer, offset).start()

    def sum_middle(layer):
        mine = pl.ds(pl.multiple_of(core * share + me * piece, 8), piece)
        total = pack[layer, mine]
        for offset in range(1, chips):
            out_copy(layer, offset).wait_recv()
            total = total + box[layer, offset]
        full[layer, core, pl.ds(pl.multiple_of(me * piece, 8), piece)] = total
        for offset in range(1, chips):
            all_copy(layer, offset).start()

    def sum_end(layer):
        for offset in range(1, chips):
            all_copy(layer, offset).wait_recv()
        back_copy(layer).start()
        back_copy(layer).wait_recv()
        for c in range(2):
            g_ref[layer, c * share : (c + 1) * share] = full[layer, c]

    fetch(0).start()
    for slot in range(8):
        product(slot)
        if slot == 0:
            pl.semaphore_wait(barrier, chips)
        if slot < 4:
            hop(0, slot).start()
    for slot in range(4):
        product(8 + slot)
    combine(0)
    for slot in range(4):
        hop(1, slot).start()
    for slot in range(4, 8):
        product(8 + slot)
    gather_rows(0)
    gram(0)
    sum_start(0)
    combine(1)
    sum_middle(0)
    sum_end(0)
    gather_rows(1)
    gram(1)
    sum_start(1)
    sum_middle(1)
    sum_end(1)

    for layer in range(LAYERS):
        for k in range(6):
            hop(layer, k).wait_send()
        pair_copy(layer).wait_send()
        back_copy(layer).wait_send()
        for offset in range(1, chips):
            out_copy(layer, offset).wait_send()
            all_copy(layer, offset).wait_send()


def fused(weights, keep, sketch, cols, chips):
    _, row_count, col_count = weights.shape
    width = sketch.shape[1]
    rows_here = row_count // cols
    half = rows_here // 2
    packed = len(upper_blocks(width)) * BLOCK
    share = packed // 2
    vmem = pl.BlockSpec(memory_space=pltpu.VMEM)
    f32 = jnp.float32
    dma = pltpu.SemaphoreType.DMA
    return pl.pallas_call(
        lambda *refs: fused_kernel(cols, chips, *refs),
        in_specs=[vmem, pl.BlockSpec(memory_space=pl.ANY), vmem],
        out_specs=[vmem, vmem],
        out_shape=[
            jax.ShapeDtypeStruct((LAYERS, rows_here, width), f32),
            jax.ShapeDtypeStruct((LAYERS, packed, BLOCK), f32),
        ],
        scratch_shapes=[
            pltpu.VMEM((2, half, col_count), jnp.bfloat16),
            pltpu.VMEM((LAYERS, 8, half, width), f32),
            pltpu.VMEM((LAYERS, 6, half, width), f32),
            pltpu.VMEM((LAYERS, packed, BLOCK), f32),
            pltpu.VMEM((LAYERS, share, BLOCK), f32),
            pltpu.VMEM((LAYERS, chips, share // chips, BLOCK), f32),
            pltpu.VMEM((LAYERS, 2, share, BLOCK), f32),
            dma((2,)),
            dma((LAYERS, 6)),
            dma((LAYERS, 6)),
            dma((LAYERS,)),
            dma((LAYERS,)),
            dma((LAYERS, chips)),
            dma((LAYERS, chips)),
            dma((LAYERS, chips)),
            dma((LAYERS, chips)),
            dma((LAYERS,)),
            dma((LAYERS,)),
        ],
        compiler_params=pltpu.CompilerParams(
            vmem_limit_bytes=56 * 2**20, collective_id=0, has_side_effects=True
        ),
        cost_estimate=pl.CostEstimate(
            flops=2 * LAYERS * row_count * col_count * width,
            bytes_accessed=2 * LAYERS * row_count * col_count,
            transcendentals=0,
        ),
        name="fused",
    )(keep, weights, sketch)


def local_gram(rows_here):
    return lax.dot_general(
        rows_here,
        rows_here,
        (((0,), (0,)), ((), ())),
        precision=lax.Precision.HIGH,
        preferred_element_type=jnp.float32,
    )


def make_body(mesh):
    rows, cols = mesh.shape["row"], mesh.shape["col"]
    chips = rows // 2 * cols

    def body(weights, pattern, sketch):
        total_rows = weights.shape[1] * rows
        width = sketch.shape[1]
        blocks = upper_blocks(width)
        keep = jnp.repeat((1 - pattern).astype(jnp.bfloat16), BLOCK, axis=2)[:, :, None, :]
        if cols == 4 and rows % 2 == 0 and (len(blocks) * BLOCK) % (2 * chips * 8) == 0:
            sampled, gram = fused(weights, keep, sketch, cols, chips)
        else:
            sampled = jnp.stack(
                [
                    lax.psum_scatter(
                        sample(weights, keep, sketch, layer), "col", scatter_dimension=0, tiled=True
                    )
                    for layer in range(LAYERS)
                ]
            )
            g = [local_gram(sampled[layer]) for layer in range(LAYERS)]
            packed = jnp.stack(
                [
                    jnp.concatenate(
                        [
                            x[i * BLOCK : (i + 1) * BLOCK, j * BLOCK : (j + 1) * BLOCK]
                            for i, j in blocks
                        ]
                    )
                    for x in g
                ]
            )
            gram = lax.psum(packed, ("row", "col"))
        return apply(sampled, invert(gram, width, total_rows))

    return body


def solution(mesh):
    return jax.shard_map(
        make_body(mesh),
        mesh=mesh,
        in_specs=(P(None, "row", "col"), P(None, "row", "col"), P("col", None)),
        out_specs=P(None, ("row", "col"), None),
        check_vma=False,
    )
```

time: 352 us -> 177 us (0.50)
  waiting for transfers between devices: 265 us -> 0 us
  Pallas kernels: 54.4 us -> 173 us
  between operations: 13.2 us -> 0.04 us
  matrix products: 8.63 us -> 0 us
  local copies, waits for them, and re-layouts: 9.63 us -> 2.38 us
    psum x1 -> x0, waiting for transfers between devices: 135 us -> none  [body(): gram = lax.psum(local_gram(rows[layer]), ('row', 'col'))]
    reduce_scatter x2 -> x0, waiting for transfers between devices: 129 us -> none  [body(): rows.append(lax.psum_scatter(part, 'col', scatter_dimension=0, tiled=True))]
    pallas_call x4 -> x2, Pallas kernels: 22.3 us -> 147 us  [the longest x1 143 us: fused(): pl.pallas_call(lambda *refs: fused_kernel(cols, chips, *refs), in_specs=[...]
    dot_general x2 -> x0, matrix products: 8.63 us -> none  [local_gram(): lax.dot_general(rows_here, rows_here, (((0,), (0,)), ((), ())), precision...]
    unnamed x16 -> x4, local copies, waits for them, and re-layouts: 9.28 us -> 1.31 us
    pallas_call x2 -> x1, Pallas kernels: 32.1 us -> 25.5 us  [invert(): pl.pallas_call(lambda *refs: inverse_kernel(total_rows, *refs), in_specs=...]
  transfers between devices with their start and end apart: 3 -> 0, of which waited for: 3 -> 0; matrix products, arithmetic and copies ran while one was open for 1% -> 0% of each run, Pallas kernels for 2% -> 0%
where the time goes in v2:
time: 177 us; the launch traced here: 176 us
  Pallas kernels  173 us (98%)
  local copies, waits for them, and re-layouts  2.38 us (1%)
    pallas_call x1, Pallas kernels, fused(): pl.pallas_call(lambda *refs: fused_kernel(cols, chips, *refs), in_specs=[...  143 us
    pallas_call x1, Pallas kernels, invert(): pl.pallas_call(lambda *refs: inverse_kernel(total_rows, *refs), in_specs=...  25.5 us
    pallas_call x1, Pallas kernels, apply(): pl.pallas_call(apply_kernel, grid=(layers, row_count // tile), in_specs=[...  4.78 us

profile of v2, /device:TPU:0, one launch (start us, length us, event | category | flops | bytes accessed | tf_op | source)
XLA Modules:
  0.0 176.0 jit_solution(13984762068271635925)
XLA Ops:
  0.0 0.7 subtract_convert_fusion
  0.7 0.1 copy.5
  0.8 0.2 broadcast_in_dim.3
  1.0 0.8 broadcast_in_dim_reshape.4.refs_0_
  1.8 142.6 %fused.1 = (f32[2,768,512]{2,1,0:T(8,128)}, f32[2,1280,128]{2,1,0:T(8,128)}) custom-call(bf16[2,24,1,1536]{3,2,1,0:T(2,128)(2,1)} %broadcast_in_dim_reshape.4.refs_0_, bf16[2,3072,1536]{2,1,0:T(8,128)(2,1)} %refs_1_.1, bf16[1536,512]{1,0:T(8,128)(2,1)} %refs_2_.1), custom_call_target="tpu_custom_call" | custom-call | flops 9663676416 | bytes 18874368 | tf_op jit(solution)/shard_map/fused/pallas_call | solution.py:389
  144.4 0.0 copy-start.1
  144.5 1.3 copy-done.1
  145.8 0.0 copy-start
  145.8 25.5 %invert.1.u_ref = f32[2,512,512]{2,1,0:T(8,128)S(1)} custom-call(f32[2,1280,128]{2,1,0:T(8,128)S(1)} %copy-done.1), custom_call_target="tpu_custom_call" | custom-call | flops 40000000000 | bytes 2097152 | tf_op jit(solution)/shard_map/invert/pallas_call | solution.py:151
  171.2 0.0 copy-done
  171.2 4.8 %apply.1 = f32[2,768,512]{2,1,0:T(8,128)} custom-call(f32[2,768,512]{2,1,0:T(8,128)S(1)} %copy-done, f32[2,512,512]{2,1,0:T(8,128)S(1)} %invert.1.u_ref), custom_call_target="tpu_custom_call" | custom-call | flops 2415919104 | bytes 6291456 | tf_op jit(solution)/shard_map/apply/pallas_call | solution.py:174
Async XLA Ops:
  144.4 1.3 copy-start.1
  145.8 25.5 %copy-start = (f32[2,768,512]{2,1,0:T(8,128)S(1)}, f32[2,768,512]{2,1,0:T(8,128)}, u32[]{:S(2)}) copy-start(f32[2,768,512]{2,1,0:T(8,128)} %get-tuple-element.7.r_ref) | copy-start | bytes 9437188

commit v3 on v2

--- a/solution.py
+++ b/solution.py
@@ -113,13 +113,13 @@
     return [(i, j) for i in range(count) for j in range(i, count)]
 
 
-def inverse_kernel(total_rows, g_ref, o_ref, a, x):
-    layers, width = a.shape[0], a.shape[1]
+def inverse_of(total_rows, g_ref, o_ref, a, x, many):
+    width = a.shape[1]
     count = width // BLOCK
-    a[...] = jnp.zeros_like(a)
-    x[...] = jnp.zeros_like(x)
-    for b, (i, j) in enumerate(upper_blocks(width)):
-        for n in range(layers):
+    for n in many:
+        a[n] = jnp.zeros((width, width), jnp.float32)
+        x[n] = jnp.zeros((width, width), jnp.float32)
+        for b, (i, j) in enumerate(upper_blocks(width)):
             a[n, i * BLOCK : (i + 1) * BLOCK, j * BLOCK : (j + 1) * BLOCK] = g_ref[
                 n, b * BLOCK : (b + 1) * BLOCK
             ]
@@ -127,23 +127,27 @@
     @pl.loop(0, count)
     def _(k):
         here = pl.ds(pl.multiple_of(k * BLOCK, BLOCK), BLOCK)
-        inners = factor_blocks([a[n, here, here] for n in range(layers)], BLOCK)
+        inners = factor_blocks([a[n, here, here] for n in many], BLOCK)
         for now in range(count):
 
             @pl.when(k == now)
             def _():
                 lo, hi = now * BLOCK, (now + 1) * BLOCK
-                for n in range(layers):
+                for n, inner in zip(many, inners):
                     if now:
-                        x[n, lo:hi, :lo] = dot3(inners[n], x[n, lo:hi, :lo], ((1,), (0,)))
-                    x[n, lo:hi, lo:hi] = inners[n]
+                        x[n, lo:hi, :lo] = dot3(inner, x[n, lo:hi, :lo], ((1,), (0,)))
+                    x[n, lo:hi, lo:hi] = inner
                     if now < count - 1:
-                        right = dot3(inners[n], a[n, lo:hi, hi:], ((1,), (0,)))
+                        right = dot3(inner, a[n, lo:hi, hi:], ((1,), (0,)))
                         a[n, hi:, hi:] -= dot3(right, right, ((0,), (0,)))
                         x[n, hi:, :hi] -= dot3(right, x[n, lo:hi, :hi], ((0,), (0,)))
 
-    for n in range(layers):
+    for n in many:
         o_ref[n] = x[n].T * jnp.float32(total_rows)
+
+
+def inverse_kernel(total_rows, g_ref, o_ref, a, x):
+    inverse_of(total_rows, g_ref, o_ref, a, x, range(a.shape[0]))
 
 
 def invert(g, width, total_rows):
@@ -200,8 +204,8 @@
 
 
 def fused_kernel(
-    cols, chips, keep_ref, w_ref, s_ref, rows_ref, g_ref,
-    wbuf, part, inbox, pack, pair, box, full,
+    cols, chips, total_rows, keep_ref, w_ref, s_ref, rows_ref, u_ref,
+    g_ref, a, x, wbuf, part, inbox, pack, pair, box, full,
     wsem, rs_send, rs_recv, pair_send, pair_recv, out_send, out_recv, all_send, all_recv,
     back_send, back_recv,
 ):
@@ -350,8 +354,8 @@
     for slot in range(4):
         product(8 + slot)
     combine(0)
-    for slot in range(4):
-        hop(1, slot).start()
+    for k in (0, 1):
+        hop(1, k).start()
     for slot in range(4, 8):
         product(8 + slot)
     gather_rows(0)
@@ -359,12 +363,16 @@
     sum_start(0)
     combine(1)
     sum_middle(0)
+    for k in (2, 3):
+        hop(1, k).start()
     sum_end(0)
+    inverse_of(total_rows, g_ref, u_ref, a, x, [0])
     gather_rows(1)
     gram(1)
     sum_start(1)
     sum_middle(1)
     sum_end(1)
+    inverse_of(total_rows, g_ref, u_ref, a, x, [1])
 
     for layer in range(LAYERS):
         for k in range(6):
@@ -376,7 +384,7 @@
             all_copy(layer, offset).wait_send()
 
 
-def fused(weights, keep, sketch, cols, chips):
+def fused(weights, keep, sketch, cols, chips, total_rows):
     _, row_count, col_count = weights.shape
     width = sketch.shape[1]
     rows_here = row_count // cols
@@ -387,14 +395,17 @@
     f32 = jnp.float32
     dma = pltpu.SemaphoreType.DMA
     return pl.pallas_call(
-        lambda *refs: fused_kernel(cols, chips, *refs),
+        lambda *refs: fused_kernel(cols, chips, total_rows, *refs),
         in_specs=[vmem, pl.BlockSpec(memory_space=pl.ANY), vmem],
         out_specs=[vmem, vmem],
         out_shape=[
             jax.ShapeDtypeStruct((LAYERS, rows_here, width), f32),
-            jax.ShapeDtypeStruct((LAYERS, packed, BLOCK), f32),
+            jax.ShapeDtypeStruct((LAYERS, width, width), f32),
         ],
         scratch_shapes=[
+            pltpu.VMEM((LAYERS, packed, BLOCK), f32),
+            pltpu.VMEM((LAYERS, width, width), f32),
+            pltpu.VMEM((LAYERS, width, width), f32),
             pltpu.VMEM((2, half, col_count), jnp.bfloat16),
             pltpu.VMEM((LAYERS, 8, half, width), f32),
             pltpu.VMEM((LAYERS, 6, half, width), f32),
@@ -446,7 +457,7 @@
         blocks = upper_blocks(width)
         keep = jnp.repeat((1 - pattern).astype(jnp.bfloat16), BLOCK, axis=2)[:, :, None, :]
         if cols == 4 and rows % 2 == 0 and (len(blocks) * BLOCK) % (2 * chips * 8) == 0:
-            sampled, gram = fused(weights, keep, sketch, cols, chips)
+            sampled, upper = fused(weights, keep, sketch, cols, chips, total_rows)
         else:
             sampled = jnp.stack(
                 [
@@ -469,7 +480,8 @@
                 ]
             )
             gram = lax.psum(packed, ("row", "col"))
-        return apply(sampled, invert(gram, width, total_rows))
+            upper = invert(gram, width, total_rows)
+        return apply(sampled, upper)
 
     return body
 

time: 177 us -> 172 us (0.972)
  Pallas kernels: 173 us -> 165 us
  local copies, waits for them, and re-layouts: 2.38 us -> 4.54 us
    pallas_call x2 -> x1, Pallas kernels: 168 us -> 160 us  [fused(): pl.pallas_call(lambda *refs: fused_kernel(cols, chips, total_rows, *refs)...]
    unnamed x4, local copies, waits for them, and re-layouts: 1.31 us -> 3.47 us
where the time goes in v3:
time: 172 us; the launch traced here: 170 us
  Pallas kernels  165 us (96%)
  local copies, waits for them, and re-layouts  4.54 us (3%)
    pallas_call x1, Pallas kernels, fused(): pl.pallas_call(lambda *refs: fused_kernel(cols, chips, total_rows, *refs)...  160 us
    pallas_call x1, Pallas kernels, apply(): pl.pallas_call(apply_kernel, grid=(layers, row_count // tile), in_specs=[...  4.74 us
    unnamed x4, local copies, waits for them, and re-layouts  3.47 us

profile of v3, /device:TPU:0, one launch (start us, length us, event | category | flops | bytes accessed | tf_op | source)
XLA Modules:
  0.0 169.8 jit_solution(15891638126220724049)
XLA Ops:
  0.0 0.7 subtract_convert_fusion
  0.7 0.1 copy.5
  0.8 0.2 broadcast_in_dim.3
  1.0 0.8 broadcast_in_dim_reshape.4.refs_0_
  1.8 159.8 %fused.1 = (f32[2,768,512]{2,1,0:T(8,128)}, f32[2,512,512]{2,1,0:T(8,128)}) custom-call(bf16[2,24,1,1536]{3,2,1,0:T(2,128)(2,1)} %broadcast_in_dim_reshape.4.refs_0_, bf16[2,3072,1536]{2,1,0:T(8,128)(2,1)} %refs_1_.1, bf16[1536,512]{1,0:T(8,128)(2,1)} %refs_2_.1), custom_call_target="tpu_custom_call" | custom-call | flops 9663676416 | bytes 18874368 | tf_op jit(solution)/shard_map/fused/pallas_call | solution.py:397
  161.6 0.0 copy-start
  161.6 1.9 %copy-done = f32[2,768,512]{2,1,0:T(8,128)S(1)} copy-done((f32[2,768,512]{2,1,0:T(8,128)S(1)}, f32[2,768,512]{2,1,0:T(8,128)}, u32[]{:S(2)}) %copy-start) | copy-done | bytes 3145752
  163.5 0.0 copy-start.1
  163.5 1.6 copy-done.1
  165.1 4.7 %apply.1 = f32[2,768,512]{2,1,0:T(8,128)} custom-call(f32[2,768,512]{2,1,0:T(8,128)S(1)} %copy-done, f32[2,512,512]{2,1,0:T(8,128)S(1)} %copy-done.1), custom_call_target="tpu_custom_call" | custom-call | flops 2415919104 | bytes 6291456 | tf_op jit(solution)/shard_map/apply/pallas_call | solution.py:178
Async XLA Ops:
  161.6 1.9 %copy-start = (f32[2,768,512]{2,1,0:T(8,128)S(1)}, f32[2,768,512]{2,1,0:T(8,128)}, u32[]{:S(2)}) copy-start(f32[2,768,512]{2,1,0:T(8,128)} %get-tuple-element.7.r_ref) | copy-start | bytes 9437188
  163.5 1.6 copy-start.1

commit v4 on v3

--- a/solution.py
+++ b/solution.py
@@ -113,7 +113,7 @@
     return [(i, j) for i in range(count) for j in range(i, count)]
 
 
-def inverse_of(total_rows, g_ref, o_ref, a, x, many):
+def inverse_of(g_ref, a, x, many):
     width = a.shape[1]
     count = width // BLOCK
     for n in many:
@@ -142,12 +142,11 @@
                         a[n, hi:, hi:] -= dot3(right, right, ((0,), (0,)))
                         x[n, hi:, :hi] -= dot3(right, x[n, lo:hi, :hi], ((0,), (0,)))
 
-    for n in many:
+
+def inverse_kernel(total_rows, g_ref, o_ref, a, x):
+    inverse_of(g_ref, a, x, range(a.shape[0]))
+    for n in range(a.shape[0]):
         o_ref[n] = x[n].T * jnp.float32(total_rows)
-
-
-def inverse_kernel(total_rows, g_ref, o_ref, a, x):
-    inverse_of(total_rows, g_ref, o_ref, a, x, range(a.shape[0]))
 
 
 def invert(g, width, total_rows):
@@ -204,9 +203,9 @@
 
 
 def fused_kernel(
-    cols, chips, total_rows, keep_ref, w_ref, s_ref, rows_ref, u_ref,
-    g_ref, a, x, wbuf, part, inbox, pack, pair, box, full,
-    wsem, rs_send, rs_recv, pair_send, pair_recv, out_send, out_recv, all_send, all_recv,
+    cols, chips, total_rows, keep_ref, w_ref, s_ref, o_ref,
+    rows_ref, basis, g_ref, a, x, wbuf, part, inbox, pack, pair, box, full,
+    osem, wsem, rs_send, rs_recv, pair_send, pair_recv, out_send, out_recv, all_send, all_recv,
     back_send, back_recv,
 ):
     row, col = lax.axis_index("row"), lax.axis_index("col")
@@ -261,36 +260,63 @@
 
     targets = [to_x, to_y, to_x, to_y, to_y, to_x]
 
-    def hop(layer, k):
+    def hop(layer, k, b):
+        here = pl.ds(b * BLOCK, BLOCK)
         return remote(
-            part.at[layer, k], inbox.at[layer, k],
-            rs_send.at[layer, k], rs_recv.at[layer, k], targets[k],
+            part.at[layer, k, here], inbox.at[layer, k, here],
+            rs_send.at[layer, k, b], rs_recv.at[layer, k, b], targets[k],
         )
 
     def combine(layer):
-        for k in (0, 1):
-            hop(layer, k).wait_recv()
-            part[layer, 4 + k] += inbox[layer, k]
-            hop(layer, 4 + k).start()
-
-    def gather_rows(layer):
-        for k in (0, 1):
-            hop(layer, 2 + k).wait_recv()
-            hop(layer, 4 + k).wait_recv()
-            rows_ref[layer, k * half : (k + 1) * half] = (
-                part[layer, 6 + k] + inbox[layer, 2 + k] + inbox[layer, 4 + k]
-            )
+        for b in range(blocks):
+            here = slice(b * BLOCK, (b + 1) * BLOCK)
+            for k in (0, 1):
+                hop(layer, k, b).wait_recv()
+                part[layer, 4 + k, here] += inbox[layer, k, here]
+                hop(layer, 4 + k, b).start()
 
     def gram(layer):
-        at = 0
-        for i in range(width // BLOCK):
-            lo = i * BLOCK
-            g = dot3(
-                rows_ref[layer, :, lo : lo + BLOCK], rows_ref[layer, :, lo:], ((0,), (0,))
-            )
-            for j in range((width - lo) // BLOCK):
-                pack[layer, at : at + BLOCK] = g[:, j * BLOCK : (j + 1) * BLOCK]
-                at += BLOCK
+        for b in range(blocks):
+            here = slice(b * BLOCK, (b + 1) * BLOCK)
+            landed = []
+            for k in (0, 1):
+                hop(layer, 2 + k, b).wait_recv()
+                hop(layer, 4 + k, b).wait_recv()
+                landed.append(
+                    part[layer, 6 + k, here] + inbox[layer, 2 + k, here] + inbox[layer, 4 + k, here]
+                )
+                first = k * half + b * BLOCK
+                rows_ref[layer, first : first + BLOCK] = landed[k]
+            y = jnp.concatenate(landed, axis=0)
+            at = 0
+            for i in range(width // BLOCK):
+                lo = i * BLOCK
+                g = dot3(y[:, lo : lo + BLOCK], y[:, lo:], ((0,), (0,)))
+                for j in range((width - lo) // BLOCK):
+                    term = g[:, j * BLOCK : (j + 1) * BLOCK]
+                    if b:
+                        term = term + pack[layer, at : at + BLOCK]
+                    pack[layer, at : at + BLOCK] = term
+                    at += BLOCK
+
+    def out(layer):
+        return pltpu.make_async_copy(basis.at[layer], o_ref.at[layer], osem.at[layer])
+
+    def finish(layer):
+        inverse_of(g_ref, a, x, [layer])
+        high, low = split(x[layer])
+        tile = 2 * BLOCK
+        for first in range(0, 2 * half, tile):
+            y_high, y_low = split(rows_ref[layer, first : first + tile])
+
+            def one(p, q):
+                return lax.dot_general(
+                    p, q, (((1,), (1,)), ((), ())), preferred_element_type=jnp.float32
+                )
+
+            solved = one(y_high, high) + (one(y_high, low) + one(y_low, high))
+            basis[layer, first : first + tile] = solved * jnp.float32(total_rows)
+        out(layer).start()
 
     def pair_copy(layer):
         other = pl.ds(pl.multiple_of((1 - core) * share, 8), share)
@@ -350,33 +376,36 @@
         if slot == 0:
             pl.semaphore_wait(barrier, chips)
         if slot < 4:
-            hop(0, slot).start()
+            for b in range(blocks):
+                hop(0, slot, b).start()
     for slot in range(4):
         product(8 + slot)
     combine(0)
-    for k in (0, 1):
-        hop(1, k).start()
+    for b in range(blocks):
+        for k in (0, 1):
+            hop(1, k, b).start()
     for slot in range(4, 8):
         product(8 + slot)
-    gather_rows(0)
     gram(0)
     sum_start(0)
     combine(1)
     sum_middle(0)
-    for k in (2, 3):
-        hop(1, k).start()
+    for b in range(blocks):
+        for k in (2, 3):
+            hop(1, k, b).start()
     sum_end(0)
-    inverse_of(total_rows, g_ref, u_ref, a, x, [0])
-    gather_rows(1)
+    finish(0)
     gram(1)
     sum_start(1)
     sum_middle(1)
     sum_end(1)
-    inverse_of(total_rows, g_ref, u_ref, a, x, [1])
+    finish(1)
 
     for layer in range(LAYERS):
         for k in range(6):
-            hop(layer, k).wait_send()
+            for b in range(blocks):
+                hop(layer, k, b).wait_send()
+        out(layer).wait()
         pair_copy(layer).wait_send()
         back_copy(layer).wait_send()
         for offset in range(1, chips):
@@ -397,12 +426,11 @@
     return pl.pallas_call(
         lambda *refs: fused_kernel(cols, chips, total_rows, *refs),
         in_specs=[vmem, pl.BlockSpec(memory_space=pl.ANY), vmem],
-        out_specs=[vmem, vmem],
-        out_shape=[
-            jax.ShapeDtypeStruct((LAYERS, rows_here, width), f32),
-            jax.ShapeDtypeStruct((LAYERS, width, width), f32),
-        ],
+        out_specs=pl.BlockSpec(memory_space=pl.ANY),
+        out_shape=jax.ShapeDtypeStruct((LAYERS, rows_here, width), f32),
         scratch_shapes=[
+            pltpu.VMEM((LAYERS, rows_here, width), f32),
+            pltpu.VMEM((LAYERS, rows_here, width), f32),
             pltpu.VMEM((LAYERS, packed, BLOCK), f32),
             pltpu.VMEM((LAYERS, width, width), f32),
             pltpu.VMEM((LAYERS, width, width), f32),
@@ -413,9 +441,10 @@
             pltpu.VMEM((LAYERS, share, BLOCK), f32),
             pltpu.VMEM((LAYERS, chips, share // chips, BLOCK), f32),
             pltpu.VMEM((LAYERS, 2, share, BLOCK), f32),
+            dma((LAYERS,)),
             dma((2,)),
-            dma((LAYERS, 6)),
-            dma((LAYERS, 6)),
+            dma((LAYERS, 6, half // BLOCK)),
+            dma((LAYERS, 6, half // BLOCK)),
             dma((LAYERS,)),
             dma((LAYERS,)),
             dma((LAYERS, chips)),
@@ -457,30 +486,29 @@
         blocks = upper_blocks(width)
         keep = jnp.repeat((1 - pattern).astype(jnp.bfloat16), BLOCK, axis=2)[:, :, None, :]
         if cols == 4 and rows % 2 == 0 and (len(blocks) * BLOCK) % (2 * chips * 8) == 0:
-            sampled, upper = fused(weights, keep, sketch, cols, chips, total_rows)
-        else:
-            sampled = jnp.stack(
-                [
-                    lax.psum_scatter(
-                        sample(weights, keep, sketch, layer), "col", scatter_dimension=0, tiled=True
-                    )
-                    for layer in range(LAYERS)
-                ]
-            )
-            g = [local_gram(sampled[layer]) for layer in range(LAYERS)]
-            packed = jnp.stack(
-                [
-                    jnp.concatenate(
-                        [
-                            x[i * BLOCK : (i + 1) * BLOCK, j * BLOCK : (j + 1) * BLOCK]
-                            for i, j in blocks
-                        ]
-                    )
-                    for x in g
-                ]
-            )
-            gram = lax.psum(packed, ("row", "col"))
-            upper = invert(gram, width, total_rows)
+            return fused(weights, keep, sketch, cols, chips, total_rows)
+        sampled = jnp.stack(
+            [
+                lax.psum_scatter(
+                    sample(weights, keep, sketch, layer), "col", scatter_dimension=0, tiled=True
+                )
+                for layer in range(LAYERS)
+            ]
+        )
+        g = [local_gram(sampled[layer]) for layer in range(LAYERS)]
+        packed = jnp.stack(
+            [
+                jnp.concatenate(
+                    [
+                        x[i * BLOCK : (i + 1) * BLOCK, j * BLOCK : (j + 1) * BLOCK]
+                        for i, j in blocks
+                    ]
+                )
+                for x in g
+            ]
+        )
+        gram = lax.psum(packed, ("row", "col"))
+        upper = invert(gram, width, total_rows)
         return apply(sampled, upper)
 
     return body

time: 172 us -> 167 us (0.971)
  Pallas kernels: 165 us -> 159 us
    pallas_call x1 -> x0, Pallas kernels: 4.74 us -> none  [apply(): pl.pallas_call(apply_kernel, grid=(layers, row_count // tile), in_specs=[...]
    unnamed x4 -> x1, local copies, waits for them, and re-layouts: 3.47 us -> 3.86 us
where the time goes in v4:
time: 167 us; the launch traced here: 165 us
  Pallas kernels  159 us (95%)
  local copies, waits for them, and re-layouts  4.93 us (3%)
    pallas_call x1, Pallas kernels, fused(): pl.pallas_call(lambda *refs: fused_kernel(cols, chips, total_rows, *refs)...  159 us
    unnamed x1, local copies, waits for them, and re-layouts  3.86 us

profile of v4, /device:TPU:0, one launch (start us, length us, event | category | flops | bytes accessed | tf_op | source)
XLA Modules:
  0.0 164.8 jit_solution(8889032272356367906)
XLA Ops:
  0.0 0.7 subtract_convert_fusion
  0.7 0.1 copy.5
  0.8 0.2 broadcast_in_dim.3
  1.0 0.8 broadcast_in_dim_reshape.4.refs_0_
  1.8 159.2 %fused.1 = f32[2,768,512]{2,1,0:T(8,128)} custom-call(bf16[2,24,1,1536]{3,2,1,0:T(2,128)(2,1)} %broadcast_in_dim_reshape.4.refs_0_, bf16[2,3072,1536]{2,1,0:T(8,128)(2,1)} %refs_1_.1, bf16[1536,512]{1,0:T(8,128)(2,1)} %refs_2_.1), custom_call_target="tpu_custom_call" | custom-call | flops 9663676416 | bytes 18874368 | tf_op jit(solution)/shard_map/fused/pallas_call | solution.py:426
  161.0 3.9 %copy.8 = f32[2,768,512]{2,1,0:T(8,128)} copy(f32[2,768,512]{2,1,0:T(8,128)} %fused.1) | data formatting | bytes 6291456

commit v5 on v4

--- a/solution.py
+++ b/solution.py
@@ -386,11 +386,13 @@
             hop(1, k, b).start()
     for slot in range(4, 8):
         product(8 + slot)
+    for k in (2, 3):
+        hop(1, k, 0).start()
     gram(0)
     sum_start(0)
     combine(1)
     sum_middle(0)
-    for b in range(blocks):
+    for b in range(1, blocks):
         for k in (2, 3):
             hop(1, k, b).start()
     sum_end(0)

time: 167 us -> 173 us (1.036)
  Pallas kernels: 159 us -> 165 us
    pallas_call x1, Pallas kernels: 159 us -> 165 us  [fused(): pl.pallas_call(lambda *refs: fused_kernel(cols, chips, total_rows, *refs)...]
where the time goes in v5:
time: 173 us; the launch traced here: 170 us
  Pallas kernels  165 us (95%)
  local copies, waits for them, and re-layouts  4.93 us (3%)
    pallas_call x1, Pallas kernels, fused(): pl.pallas_call(lambda *refs: fused_kernel(cols, chips, total_rows, *refs)...  165 us
    unnamed x1, local copies, waits for them, and re-layouts  3.86 us

profile of v5, /device:TPU:0, one launch (start us, length us, event | category | flops | bytes accessed | tf_op | source)
XLA Modules:
  0.0 170.5 jit_solution(1758422706936224010)
XLA Ops:
  0.0 0.7 subtract_convert_fusion
  0.7 0.1 copy.5
  0.8 0.2 broadcast_in_dim.3
  1.0 0.8 broadcast_in_dim_reshape.4.refs_0_
  1.8 164.8 %fused.1 = f32[2,768,512]{2,1,0:T(8,128)} custom-call(bf16[2,24,1,1536]{3,2,1,0:T(2,128)(2,1)} %broadcast_in_dim_reshape.4.refs_0_, bf16[2,3072,1536]{2,1,0:T(8,128)(2,1)} %refs_1_.1, bf16[1536,512]{1,0:T(8,128)(2,1)} %refs_2_.1), custom_call_target="tpu_custom_call" | custom-call | flops 9663676416 | bytes 18874368 | tf_op jit(solution)/shard_map/fused/pallas_call | solution.py:428
  166.6 3.9 %copy.8 = f32[2,768,512]{2,1,0:T(8,128)} copy(f32[2,768,512]{2,1,0:T(8,128)} %fused.1) | data formatting | bytes 6291456
